TPU v7x, 32 devices: a whole 2x2x4 slice. The times are simulated.
32 devices in a mesh: dp: 16 (over z, x, core), tensor: 2 (over y).
Axes of the slice: x: 2, y: 2, z: 4, core: 2. Of those that a mesh axis runs over, the one named last changes fastest.
Arguments:
- tokens: bfloat16 [8192, 2048], P(('dp', 'tensor')), may hold values from -6 to 6
- lengths: int32 [16, 2], P('dp'), may hold values from 0 to 512, as said below
- w_qkv: bfloat16 [2048, 8, 768], P('dp', 'tensor'), may hold values from -0.125 to 0.125
- b_qkv: float32 [8, 768], P('tensor'), may hold values from -2 to 2
- w_out: bfloat16 [2048, 8, 256], P('dp', 'tensor'), may hold values from -0.75 to 0.75
- b_out: float32 [2048], replicated, may hold values from -2 to 2
- w_fc: bfloat16 [2048, 8192], P('dp', 'tensor'), may hold values from -0.125 to 0.125
- b_fc: float32 [8192], P('tensor'), may hold values from -2 to 2
- w_proj: bfloat16 [2048, 8192], P('dp', 'tensor'), may hold values from -0.0625 to 0.0625
- b_proj: float32 [2048], replicated, may hold values from -2 to 2
- gain_attn: float32 [2048], replicated, may hold values from 0.5 to 1.5
- shift_attn: float32 [2048], replicated, may hold values from -2 to 2
- gain_mlp: float32 [2048], replicated, may hold values from 0.5 to 1.5
- shift_mlp: float32 [2048], replicated, may hold values from -2 to 2
- cotangent: bfloat16 [8192, 2048], P(('dp', 'tensor')), may hold values from -6 to 6
Outputs:
- output: bfloat16 [8192, 2048], P(('dp', 'tensor'))
- grad_tokens: bfloat16 [8192, 2048], P(('dp', 'tensor'))
- grad_w_qkv: float32 [2048, 8, 768], P('dp', 'tensor')
- grad_b_qkv: float32 [8, 768], P('tensor')
- grad_w_out: float32 [2048, 8, 256], P('dp', 'tensor')
- grad_b_out: float32 [2048], replicated
- grad_w_fc: float32 [2048, 8192], P('dp', 'tensor')
- grad_b_fc: float32 [8192], P('tensor')
- grad_w_proj: float32 [2048, 8192], P('dp', 'tensor')
- grad_b_proj: float32 [2048], replicated
- grad_gain_attn: float32 [2048], replicated
- grad_shift_attn: float32 [2048], replicated
- grad_gain_mlp: float32 [2048], replicated
- grad_shift_mlp: float32 [2048], replicated
Inputs may be any that keep to these rules, and one draw needn't show every extreme that they name: Row g holds the lengths of the two sequences packed from the first row of data group g; the first is longer than 256, both together are at most 512, the remaining rows are padding, and in one group drawn from the seed the first sequence fills all 512 rows.
All inputs are finite; a program needn't handle non-finite values.
Results may differ from a plain program's by a relative error of at most 0.011.
Values may be sent and summed in bfloat16 or wider, within the bound.
A program may use at most 256 MiB of HBM per device.

v0:
```python
import math

import jax
import jax.numpy as jnp
from jax import lax
from jax.sharding import PartitionSpec as P

HEAD = 256
ROT = 64


def layout(length_row, row_index):
    first_len = length_row[0]
    both_len = first_len + length_row[1]
    segment = (row_index >= first_len).astype(jnp.int32) + (row_index >= both_len).astype(jnp.int32)
    begin = jnp.where(segment == 0, 0, jnp.where(segment == 1, first_len, both_len))
    return (segment, (row_index - begin).astype(jnp.float32))


def angles(position):
    freq_index = jnp.arange(ROT // 2, dtype=jnp.float32) * (2.0 / ROT)
    inverse = jnp.exp(freq_index * -math.log(10000.0))
    phase_angle = position[:, None] * inverse[None, :]
    return (jnp.cos(phase_angle)[:, None, :], jnp.sin(phase_angle)[:, None, :])


def rotary(vector, cosine, sine_part):
    half_rot = ROT // 2
    lower_part = vector[..., :half_rot]
    upper_part = vector[..., half_rot:ROT]
    return jnp.concatenate(
        [
            lower_part * cosine - upper_part * sine_part,
            upper_part * cosine + lower_part * sine_part,
            vector[..., ROT:],
        ],
        axis=-1,
    )


def normalize(vector, gain_vec, shift_vec):
    center = vector - jnp.mean(vector, axis=-1, keepdims=True)
    spread = jnp.mean(center * center, axis=-1, keepdims=True)
    inv_dev = lax.rsqrt(spread + 1e-05)
    scaled = center * inv_dev
    return (scaled * gain_vec + shift_vec, scaled, inv_dev)


def norm_back(grad_out, scaled, inv_dev, gain_vec):
    grad_scaled = grad_out * gain_vec
    return inv_dev * (
        grad_scaled
        - jnp.mean(grad_scaled, axis=-1, keepdims=True)
        - scaled * jnp.mean(grad_scaled * scaled, axis=-1, keepdims=True)
    )


def gelu_slope(vector):
    return 0.5 * (1.0 + jax.scipy.special.erf(vector * (1.0 / math.sqrt(2.0)))) + vector * jnp.exp(
        -0.5 * vector * vector
    ) * (1.0 / math.sqrt(2.0 * math.pi))


def local(
    tokens,
    lengths,
    w_qkv,
    b_qkv,
    w_out,
    b_out,
    w_fc,
    b_fc,
    w_proj,
    b_proj,
    gain_attn,
    shift_attn,
    gain_mlp,
    shift_mlp,
    cotangent,
):
    shard_rows = tokens.shape[0]
    group_rows = shard_rows * lax.axis_size("tensor")
    row_index = jnp.arange(group_rows, dtype=jnp.int32)
    segment, position = layout(lengths[0], row_index)
    own_index = lax.axis_index("tensor") * shard_rows + jnp.arange(shard_rows, dtype=jnp.int32)
    own_segment = layout(lengths[0], own_index)[0]
    own_live = (own_segment < 2).astype(jnp.float32)[:, None]
    cosine, sine_part = angles(position)
    residual = tokens.astype(jnp.float32)
    normed_one, scaled_one, inv_one = normalize(residual, gain_attn, shift_attn)
    normed_two, scaled_two, inv_two = normalize(residual, gain_mlp, shift_mlp)
    normed_attn, normed_mlp = (
        lax.all_gather(normed_one.astype(jnp.bfloat16), "tensor", axis=0, tiled=True),
        lax.all_gather(normed_two.astype(jnp.bfloat16), "tensor", axis=0, tiled=True),
    )
    full_qkv, full_out, full_fc, full_proj = (
        lax.all_gather(w_qkv, "dp", axis=0, tiled=True),
        lax.all_gather(w_out, "dp", axis=0, tiled=True),
        lax.all_gather(w_fc, "dp", axis=0, tiled=True),
        lax.all_gather(w_proj, "dp", axis=0, tiled=True),
    )
    joined_qkv = (
        jnp.einsum("td,dhe->the", normed_attn, full_qkv, preferred_element_type=jnp.float32) + b_qkv
    )
    queries = rotary(joined_qkv[..., :HEAD], cosine, sine_part).astype(jnp.bfloat16)
    key_rot = rotary(joined_qkv[..., HEAD : 2 * HEAD], cosine, sine_part).astype(jnp.bfloat16)
    values = joined_qkv[..., 2 * HEAD :].astype(jnp.bfloat16)
    scale_factor = 1.0 / math.sqrt(HEAD)
    scores = (
        jnp.einsum("qhe,khe->hqk", queries, key_rot, preferred_element_type=jnp.float32)
        * scale_factor
    )
    allowed = (segment[:, None] == segment[None, :]) & (row_index[:, None] >= row_index[None, :])
    scores = jnp.where(allowed[None], scores, -1e30)
    shifted = jnp.exp(scores - jnp.max(scores, axis=-1, keepdims=True))
    attn_probs = shifted / jnp.sum(shifted, axis=-1, keepdims=True)
    probs_low = attn_probs.astype(jnp.bfloat16)
    mixed_heads = jnp.einsum(
        "hqk,khe->qhe", probs_low, values, preferred_element_type=jnp.float32
    ).astype(jnp.bfloat16)
    attended = jnp.einsum("qhe,dhe->qd", mixed_heads, full_out, preferred_element_type=jnp.float32)
    hidden_pre = jnp.dot(normed_mlp, full_fc, preferred_element_type=jnp.float32) + b_fc
    hidden = jax.nn.gelu(hidden_pre, approximate=False).astype(jnp.bfloat16)
    projected = jnp.einsum("tf,df->td", hidden, full_proj, preferred_element_type=jnp.float32)
    branch_own = lax.psum_scatter(attended + projected, "tensor", scatter_dimension=0, tiled=True)
    output = (residual + own_live * (branch_own + b_out + b_proj)).astype(jnp.bfloat16)
    cot_float = cotangent.astype(jnp.float32)
    grad_own = cot_float * own_live
    grad_branch = lax.all_gather(grad_own.astype(jnp.bfloat16), "tensor", axis=0, tiled=True)
    full_qkv, full_out, full_fc, full_proj = (
        lax.all_gather(w_qkv, "dp", axis=0, tiled=True),
        lax.all_gather(w_out, "dp", axis=0, tiled=True),
        lax.all_gather(w_fc, "dp", axis=0, tiled=True),
        lax.all_gather(w_proj, "dp", axis=0, tiled=True),
    )
    grad_hidden = jnp.einsum(
        "td,df->tf", grad_branch, full_proj, preferred_element_type=jnp.float32
    )
    grad_pre = (grad_hidden * gelu_slope(hidden_pre)).astype(jnp.bfloat16)
    grad_proj = jnp.einsum("td,tf->df", grad_branch, hidden, preferred_element_type=jnp.float32)
    grad_fc = jnp.einsum("td,tf->df", normed_mlp, grad_pre, preferred_element_type=jnp.float32)
    grad_bias_fc = jnp.sum(grad_pre.astype(jnp.float32), axis=0)
    grad_normed_mlp = jnp.einsum("tf,df->td", grad_pre, full_fc, preferred_element_type=jnp.float32)
    grad_mixed = jnp.einsum(
        "td,dhe->the", grad_branch, full_out, preferred_element_type=jnp.float32
    ).astype(jnp.bfloat16)
    grad_out = jnp.einsum(
        "td,the->dhe", grad_branch, mixed_heads, preferred_element_type=jnp.float32
    )
    grad_probs = jnp.einsum("qhe,khe->hqk", grad_mixed, values, preferred_element_type=jnp.float32)
    grad_scores = (
        attn_probs * (grad_probs - jnp.sum(attn_probs * grad_probs, axis=-1, keepdims=True))
    ).astype(jnp.bfloat16)
    grad_values = jnp.einsum(
        "hqk,qhe->khe", probs_low, grad_mixed, preferred_element_type=jnp.float32
    )
    grad_queries = (
        jnp.einsum("hqk,khe->qhe", grad_scores, key_rot, preferred_element_type=jnp.float32)
        * scale_factor
    )
    grad_keys = (
        jnp.einsum("hqk,qhe->khe", grad_scores, queries, preferred_element_type=jnp.float32)
        * scale_factor
    )
    grad_joined = jnp.concatenate(
        [
            rotary(grad_queries, cosine, -sine_part),
            rotary(grad_keys, cosine, -sine_part),
            grad_values,
        ],
        axis=-1,
    ).astype(jnp.bfloat16)
    grad_bias_qkv = jnp.sum(grad_joined.astype(jnp.float32), axis=0)
    grad_qkv = jnp.einsum(
        "td,the->dhe", normed_attn, grad_joined, preferred_element_type=jnp.float32
    )
    grad_normed_attn = jnp.einsum(
        "the,dhe->td", grad_joined, full_qkv, preferred_element_type=jnp.float32
    )
    own_attn, own_mlp = (
        lax.psum_scatter(grad_normed_attn, "tensor", scatter_dimension=0, tiled=True),
        lax.psum_scatter(grad_normed_mlp, "tensor", scatter_dimension=0, tiled=True),
    )
    grad_tokens = (
        cot_float
        + norm_back(own_attn, scaled_one, inv_one, gain_attn)
        + norm_back(own_mlp, scaled_two, inv_two, gain_mlp)
    )
    summed_qkv, summed_out, summed_fc, summed_proj = (
        lax.psum_scatter(grad_qkv, "dp", scatter_dimension=0, tiled=True),
        lax.psum_scatter(grad_out, "dp", scatter_dimension=0, tiled=True),
        lax.psum_scatter(grad_fc, "dp", scatter_dimension=0, tiled=True),
        lax.psum_scatter(grad_proj, "dp", scatter_dimension=0, tiled=True),
    )
    bias_qkv, bias_fc = lax.psum((grad_bias_qkv, grad_bias_fc), "dp")
    column_sums = lax.psum(
        (
            jnp.sum(grad_own, axis=0),
            jnp.sum(own_attn * scaled_one, axis=0),
            jnp.sum(own_attn, axis=0),
            jnp.sum(own_mlp * scaled_two, axis=0),
            jnp.sum(own_mlp, axis=0),
        ),
        ("dp", "tensor"),
    )
    return (
        output,
        grad_tokens.astype(jnp.bfloat16),
        summed_qkv,
        bias_qkv,
        summed_out,
        column_sums[0],
        summed_fc,
        bias_fc,
        summed_proj,
        column_sums[0],
        column_sums[1],
        column_sums[2],
        column_sums[3],
        column_sums[4],
    )


def solution(mesh):
    placed = (
        P(("dp", "tensor"), None),
        P("dp", None),
        P("dp", "tensor", None),
        P("tensor", None),
        P("dp", "tensor", None),
        P(),
        P("dp", "tensor"),
        P("tensor"),
        P("dp", "tensor"),
        P(),
        P(),
        P(),
        P(),
        P(),
        P(("dp", "tensor"), None),
    )
    return jax.shard_map(
        local,
        mesh=mesh,
        in_specs=placed,
        out_specs=(
            P(("dp", "tensor"), None),
            P(("dp", "tensor"), None),
            P("dp", "tensor", None),
            P("tensor", None),
            P("dp", "tensor", None),
            P(),
            P("dp", "tensor"),
            P("tensor"),
            P("dp", "tensor"),
            P(),
            P(),
            P(),
            P(),
            P(),
        ),
        check_vma=False,
    )
```

profile of v0, /device:TPU:0, one launch (start us, length us, event | category | flops | bytes accessed | tf_op | source)
XLA Modules:
  0.0 1737.3 jit_solution(39171544121568181)
XLA Ops:
  10.5 3.3 fusion.33
  26.2 23.7 %all-gather.8.cloned.1.call-done = bf16[512,2048]{1,0:T(8,128)(2,1)} async-done(((bf16[256,2048]{1,0:T(8,128)(2,1)}), bf16[512,2048]{1,0:T(8,128)(2,1)}) %all-gather.8.cloned.1.call-update) | async-done | bytes 2097168 | tf_op jit(solution)/shard_map/all_gather | solution.py:93
  49.9 103.7 %all-gather.10.cloned.1.call-done = bf16[2048,4,768]{2,0,1:T(8,128)(2,1)} async-done(((bf16[128,4,768]{2,0,1:T(8,128)(2,1)}), bf16[2048,4,768]{2,0,1:T(8,128)(2,1)}) %all-gather.10.cloned.1.call-update) | async-done | bytes 12582928 | tf_op jit(solution)/shard_map/all_gather | solution.py:97
  153.5 10.2 fusion.76
  166.7 6.2 fusion.77
  172.9 4.3 fusion.59
  177.2 9.9 all-gather.20.cloned.1.call-done
  187.0 7.6 fusion.46
  194.8 44.8 %all-gather.12.cloned.1.call-done = bf16[2048,4,256]{2,0,1:T(8,128)(2,1)} async-done(((bf16[128,4,256]{2,0,1:T(8,128)(2,1)}), bf16[2048,4,256]{2,0,1:T(8,128)(2,1)}) %all-gather.12.cloned.1.call-update) | async-done | bytes 4194320 | tf_op jit(solution)/shard_map/all_gather | solution.py:98
  239.7 5.3 fusion.56
  264.8 3.4 fusion.61
  268.2 12.2 convolution_bitcast_fusion
  280.5 121.7 %all-gather.16.cloned.1.call-done = bf16[2048,4096]{1,0:T(8,128)(2,1)} async-done(((bf16[128,4096]{1,0:T(8,128)(2,1)}), bf16[2048,4096]{1,0:T(8,128)(2,1)}) %all-gather.16.cloned.1.call-update) | async-done | bytes 16777232 | tf_op jit(solution)/shard_map/all_gather | solution.py:99
  402.2 31.1 %fusion.3 = (bf16[512,4096]{1,0:T(8,128)(2,1)}, f32[512,4096]{1,0:T(8,128)}) fusion(f32[4096]{0:T(1024)S(1)} %copy-done.27, bf16[512,2048]{1,0:T(8,128)(2,1)} %all-gather.14.cloned.1.call-done, bf16[2048,4096]{1,0:T(8,128)(2,1)} %all-gather.16.cloned.1.call-done), kind=kOutput, calls=%fused_computation.5 | convolution fusion | flops 8728346624 | bytes 31473664 | tf_op jit(solution)/shard_map/dot_general | solution.py:122
  433.3 96.1 %all-gather.18.cloned.1.call-done = bf16[2048,4096]{1,0:T(8,128)(2,1)} async-done(((bf16[128,4096]{1,0:T(8,128)(2,1)}), bf16[2048,4096]{1,0:T(8,128)(2,1)}) %all-gather.18.cloned.1.call-update) | async-done | bytes 16777232 | tf_op jit(solution)/shard_map/all_gather | solution.py:100
  529.4 16.6 convert_reduce_fusion
  548.1 15.1 fusion.79
  563.2 5.0 fusion.78
  568.3 15.1 bitcast_add_fusion
  583.4 13.8 fusion.50
  598.8 18.0 %fusion.80 = f32[2048,4096]{1,0:T(8,128)} fusion(bf16[512,2048]{1,0:T(8,128)(2,1)S(1)} %copy-done.26, bf16[512,4096]{1,0:T(8,128)(2,1)} %copy-done.29), kind=kOutput, calls=%fused_computation.143 | convolution fusion | flops 8589934592 | bytes 39845888 | tf_op jit(solution)/shard_map/td,tf->df/dot_general | solution.py:141
  618.4 17.9 %fusion.81 = f32[2048,4096]{1,0:T(8,128)} fusion(bf16[512,2048]{1,0:T(8,128)(2,1)S(1)} %copy-done.25, bf16[512,4096]{1,0:T(8,128)(2,1)} %get-tuple-element.76), kind=kOutput, calls=%fused_computation.144 | convolution fusion | flops 8589934592 | bytes 39845888 | tf_op jit(solution)/shard_map/td,tf->df/dot_general | solution.py:140
  638.9 58.3 %all-reduce.1 = (f32[4,768]{1,0:T(4,128)}, f32[4096]{0:T(1024)}) all-reduce(f32[4,768]{1,0:T(4,128)S(1)} %convert_reduce_fusion.1, f32[4096]{0:T(1024)S(1)} %get-tuple-element.78), channel_id=1, replica_groups=mesh['dp'=16,'tensor'=2] {'dp'}, use_global_device_ids=true, to_apply=%region_14.15 | all-reduce | flops 7168 | bytes 57344 | tf_op jit(solution)/shard_map/psum | solution.py:195
  699.4 50.0 %reduce-scatter.12.cloned.1.call-done = f32[256,2048]{1,0:T(8,128)} async-done(((f32[512,2048]{1,0:T(8,128)}), f32[256,2048]{1,0:T(8,128)}) %reduce-scatter.12.cloned.1.call-update) | async-done | bytes 2097168 | tf_op jit(solution)/shard_map/reduce_scatter | solution.py:182
  749.4 4.0 fusion.42
  753.4 40.9 %all-reduce = (f32[2048]{0:T(1024)S(1)}, f32[2048]{0:T(1024)}, f32[2048]{0:T(1024)}, f32[2048]{0:T(1024)}, f32[2048]{0:T(1024)}) all-reduce(f32[2048]{0:T(1024)S(1)} %copy-done.14, f32[2048]{0:T(1024)S(1)} %get-tuple-element.30, f32[2048]{0:T(1024)S(1)} %get-tuple-element.35, ...), channel_id=1, replica_groups=mesh['dp'=16,'tensor'=2] {'dp','tensor'}, use_global_device_ids=true, to_apply=%region_17.18 | all-reduce | flops 10240 | bytes 81920 | tf_op jit(solution)/shard_map/psum | solution.py:196
  794.4 13.0 reduce-scatter.8.cloned.1.call-done
  807.4 4.5 fusion.41
  811.9 243.7 %reduce-scatter.14.cloned.1.call-done = f32[128,4,768]{2,0,1:T(8,128)} async-done(((f32[2048,4,768]{2,0,1:T(8,128)}), f32[128,4,768]{2,0,1:T(8,128)}) %reduce-scatter.14.cloned.1.call-update) | async-done | bytes 1572880 | tf_op jit(solution)/shard_map/reduce_scatter | solution.py:190
  1055.6 3.6 copy.53
  1059.2 333.7 %reduce-scatter.18.cloned.1.call-done = f32[128,4096]{1,0:T(8,128)} async-done(((f32[2048,4096]{1,0:T(8,128)}), f32[128,4096]{1,0:T(8,128)}) %reduce-scatter.18.cloned.1.call-update) | async-done | bytes 2097168 | tf_op jit(solution)/shard_map/reduce_scatter | solution.py:192
  1392.9 337.0 %reduce-scatter.20.cloned.1.call-done = f32[128,4096]{1,0:T(8,128)} async-done(((f32[2048,4096]{1,0:T(8,128)}), f32[128,4096]{1,0:T(8,128)}) %reduce-scatter.20.cloned.1.call-update) | async-done | bytes 2097168 | tf_op jit(solution)/shard_map/reduce_scatter | solution.py:193
  (134 shorter events, 47.6 us)
Async XLA Ops:
  7.2 7.8 copy-start.24
  7.2 10.4 copy-start.3
  7.2 42.7 %all-gather.8.cloned.1.call-start = ((), (), s32[]{:S(2)}) async-start(), calls=%async_computation.7 | async-start | bytes 3145728 | tf_op jit(solution)/shard_map/all_gather | solution.py:93
  10.5 9.0 copy-start.11
  13.9 139.6 %all-gather.10.cloned.1.call-start = ((), (), s32[]{:S(2)}) async-start(), calls=%async_computation.8 | async-start | bytes 13369344 | tf_op jit(solution)/shard_map/all_gather | solution.py:97
  14.9 138.6 %copy-start.28 = (f32[4,768]{1,0:T(4,128)S(1)}, f32[4,768]{1,0:T(4,128)}, u32[]{:S(2)}) copy-start(f32[4,768]{1,0:T(4,128)} %param.18) | copy-start | bytes 36868
  14.9 172.1 %all-gather.20.cloned.1.call-start = ((), (), s32[]{:S(2)}) async-start(), calls=%async_computation.14 | async-start | bytes 3145728 | tf_op jit(solution)/shard_map/all_gather | solution.py:129
  17.6 146.2 %copy-start.19 = (f32[256]{0:T(256)}, f32[256]{0:T(256)S(1)}, u32[]{:S(2)}) copy-start(f32[256]{0:T(256)S(1)} %compare_convert_fusion) | copy-start | bytes 3076
  19.5 220.2 %all-gather.12.cloned.1.call-start = ((), (), s32[]{:S(2)}) async-start(), calls=%async_computation.9 | async-start | bytes 4456448 | tf_op jit(solution)/shard_map/all_gather | solution.py:98
  20.3 260.2 %all-gather.14.cloned.1.call-start = ((), (), s32[]{:S(2)}) async-start(), calls=%async_computation.10 | async-start | bytes 3145728 | tf_op jit(solution)/shard_map/all_gather | solution.py:94
  20.9 381.3 %all-gather.16.cloned.1.call-start = ((), (), s32[]{:S(2)}) async-start(), calls=%async_computation.11 | async-start | bytes 17825792 | tf_op jit(solution)/shard_map/all_gather | solution.py:99
  21.4 508.0 %all-gather.18.cloned.1.call-start = ((), (), s32[]{:S(2)}) async-start(), calls=%async_computation.12 | async-start | bytes 17825792 | tf_op jit(solution)/shard_map/all_gather | solution.py:100
  22.2 675.0 %reduce-scatter.16.cloned.1.call-start = ((), (), s32[]{:S(2)}) async-start(), calls=%async_computation.18 | async-start | bytes 8912896 | tf_op jit(solution)/shard_map/reduce_scatter | solution.py:191
  194.6 504.8 %reduce-scatter.10.cloned.1.call-start = ((), (), s32[]{:S(2)}) async-start(), calls=%async_computation.15 | async-start | bytes 6291456 | tf_op jit(solution)/shard_map/reduce_scatter | solution.py:181
  268.2 315.2 %copy-start.4 = (bf16[512,4,768]{0,2,1:T(8,128)(2,1)}, bf16[512,4,768]{0,2,1:T(8,128)(2,1)S(1)}, u32[]{:S(2)}) copy-start(bf16[512,4,768]{0,2,1:T(8,128)(2,1)S(1)} %fusion.61) | copy-start | bytes 9437188
  280.4 121.8 %copy-start.27 = (f32[4096]{0:T(1024)S(1)}, f32[4096]{0:T(1024)}, u32[]{:S(2)}) copy-start(f32[4096]{0:T(1024)} %param.22) | copy-start | bytes 49156
  280.4 468.9 %reduce-scatter.12.cloned.1.call-start = ((), (), s32[]{:S(2)}) async-start(), calls=%async_computation.16 | async-start | bytes 6291456 | tf_op jit(solution)/shard_map/reduce_scatter | solution.py:182
  563.2 244.2 %reduce-scatter.8.cloned.1.call-start = ((), (), s32[]{:S(2)}) async-start(), calls=%async_computation.13 | async-start | bytes 6291456 | tf_op jit(solution)/shard_map/reduce_scatter | solution.py:125
  583.4 472.3 %reduce-scatter.14.cloned.1.call-start = ((), (), s32[]{:S(2)}) async-start(), calls=%async_computation.17 | async-start | bytes 26738688 | tf_op jit(solution)/shard_map/reduce_scatter | solution.py:190
  597.3 795.6 %reduce-scatter.18.cloned.1.call-start = ((), (), s32[]{:S(2)}) async-start(), calls=%async_computation.19 | async-start | bytes 35651584 | tf_op jit(solution)/shard_map/reduce_scatter | solution.py:192
  616.8 1113.1 %reduce-scatter.20.cloned.1.call-start = ((), (), s32[]{:S(2)}) async-start(), calls=%async_computation.20 | async-start | bytes 35651584 | tf_op jit(solution)/shard_map/reduce_scatter | solution.py:193
  636.3 113.0 %copy-start = (bf16[256,2048]{1,0:T(8,128)(2,1)S(1)}, bf16[256,2048]{1,0:T(8,128)(2,1)}, u32[]{:S(2)}) copy-start(bf16[256,2048]{1,0:T(8,128)(2,1)} %param.15) | copy-start | bytes 3145732
  636.3 113.0 %copy-start.12 = (f32[2048]{0:T(1024)S(1)}, f32[2048]{0:T(1024)}, u32[]{:S(2)}) copy-start(f32[2048]{0:T(1024)} %param.27) | copy-start | bytes 24580
  636.4 113.0 %copy-start.13 = (f32[2048]{0:T(1024)S(1)}, f32[2048]{0:T(1024)}, u32[]{:S(2)}) copy-start(f32[2048]{0:T(1024)} %param.25) | copy-start | bytes 24580
  636.4 113.0 %copy-start.16 = (f32[256]{0:T(256)S(1)}, f32[256]{0:T(256)}, u32[]{:S(2)}) copy-start(f32[256]{0:T(256)} %copy-done.15) | copy-start | bytes 3076
  636.4 113.0 %copy-start.18 = (f32[256]{0:T(256)S(1)}, f32[256]{0:T(256)}, u32[]{:S(2)}) copy-start(f32[256]{0:T(256)} %copy-done.17) | copy-start | bytes 3076
  636.4 117.0 %copy-start.14 = (f32[2048]{0:T(1024)S(1)}, f32[2048]{0:T(1024)}, u32[]{:S(2)}) copy-start(f32[2048]{0:T(1024)} %get-tuple-element.59) | copy-start | bytes 24580
  636.4 171.0 %copy-start.20 = (f32[256]{0:T(256)S(1)}, f32[256]{0:T(256)}, u32[]{:S(2)}) copy-start(f32[256]{0:T(256)} %copy-done.19) | copy-start | bytes 3076
  636.4 171.0 %copy-start.22 = (f32[2048]{0:T(1024)S(1)}, f32[2048]{0:T(1024)}, u32[]{:S(2)}) copy-start(f32[2048]{0:T(1024)} %param.24) | copy-start | bytes 24580
  636.4 171.0 %copy-start.23 = (f32[2048]{0:T(1024)S(1)}, f32[2048]{0:T(1024)}, u32[]{:S(2)}) copy-start(f32[2048]{0:T(1024)} %param.20) | copy-start | bytes 24580
  699.4 108.0 %copy-start.1 = (f32[256,2048]{1,0:T(8,128)S(1)}, f32[256,2048]{1,0:T(8,128)}, u32[]{:S(2)}) copy-start(f32[256,2048]{1,0:T(8,128)} %reduce-scatter.10.cloned.1.call-done) | copy-start | bytes 6291460
  794.4 935.6 %copy-start.21 = (f32[2048]{0:T(1024)}, f32[2048]{0:T(1024)S(1)}, u32[]{:S(2)}) copy-start(f32[2048]{0:T(1024)S(1)} %get-tuple-element.105) | copy-start | bytes 24580
  (13 other events, 34.4 us)
Sparse Core Ops, SparseCore 0:
  14.0 35.8 all-gather.7
  52.7 100.7 all-gather.9
  155.7 31.2 all-gather.19
  189.1 50.5 all-gather.11
  241.6 31.5 all-gather.13
  275.3 126.8 all-gather.15
  404.4 124.9 all-gather.17
  533.5 102.8 reduce-scatter.15
  638.7 54.0 reduce-scatter.9
  695.0 54.3 reduce-scatter.11
  751.6 55.7 reduce-scatter.7
  811.9 243.6 reduce-scatter.13
  1061.1 331.7 reduce-scatter.17
  1398.1 331.7 reduce-scatter.19
where the time goes:
time: 1740 us
  waiting for transfers between devices  1380 us (79%)
  matrix products  187 us (11%)
  blocking collectives  99.2 us (6%)
  other arithmetic  28.1 us (2%)
  local copies, waits for them, and re-layouts  26.5 us (2%)
    reduce_scatter x1, waiting for transfers between devices, local(): lax.psum_scatter(grad_proj, 'dp', scatter_dimension=0, tiled=True)  337 us
    reduce_scatter x1, waiting for transfers between devices, local(): lax.psum_scatter(grad_fc, 'dp', scatter_dimension=0, tiled=True)  334 us
    reduce_scatter x1, waiting for transfers between devices, local(): lax.psum_scatter(grad_qkv, 'dp', scatter_dimension=0, tiled=True)  244 us
    all_gather x1, waiting for transfers between devices, local(): lax.all_gather(w_fc, 'dp', axis=0, tiled=True)  122 us
    all_gather x1, waiting for transfers between devices, local(): lax.all_gather(w_qkv, 'dp', axis=0, tiled=True)  104 us
    all_gather x1, waiting for transfers between devices, local(): lax.all_gather(w_proj, 'dp', axis=0, tiled=True)  96.1 us
    psum x1, blocking collectives, local(): bias_qkv, bias_fc = lax.psum((grad_bias_qkv, grad_bias_fc), 'dp')  58.3 us
    reduce_scatter x1, waiting for transfers between devices, local(): lax.psum_scatter(grad_normed_mlp, 'tensor', scatter_dimension=0, tiled=True)  50 us
  transfers between devices with their start and end apart: 14, of which 11 were waited for; matrix products, arithmetic and copies ran while one was open for 13% of the time, Pallas kernels for 0%

commit v1 on v0

v1 whole, which is shorter than its diff:
```python
import math

import jax
import jax.numpy as jnp
from jax import lax
from jax.sharding import Mesh
from jax.sharding import PartitionSpec as P

HEAD = 256
ROT = 64
INNER = 4
CHUNKS = 4
F32 = jnp.float32
BF16 = jnp.bfloat16


def layout(length_row, row_index):
    first_len = length_row[0]
    both_len = first_len + length_row[1]
    segment = (row_index >= first_len).astype(jnp.int32) + (row_index >= both_len).astype(jnp.int32)
    begin = jnp.where(segment == 0, 0, jnp.where(segment == 1, first_len, both_len))
    return (segment, (row_index - begin).astype(F32))


def angles(position):
    freq_index = jnp.arange(ROT // 2, dtype=F32) * (2.0 / ROT)
    inverse = jnp.exp(freq_index * -math.log(10000.0))
    phase_angle = position[..., None] * inverse
    return (jnp.cos(phase_angle), jnp.sin(phase_angle))


def rotary(vector, cosine, sine_part):
    half_rot = ROT // 2
    lower_part = vector[..., :half_rot]
    upper_part = vector[..., half_rot:ROT]
    return jnp.concatenate(
        [
            lower_part * cosine - upper_part * sine_part,
            upper_part * cosine + lower_part * sine_part,
            vector[..., ROT:],
        ],
        axis=-1,
    )


def norm_stats(residual):
    center = residual - jnp.mean(residual, axis=-1, keepdims=True)
    spread = jnp.mean(center * center, axis=-1, keepdims=True)
    inv_dev = lax.rsqrt(spread + 1e-05)
    return center * inv_dev, inv_dev


def gelu_slope(vector):
    return 0.5 * (1.0 + lax.erf(vector * (1.0 / math.sqrt(2.0)))) + vector * jnp.exp(
        -0.5 * vector * vector
    ) * (1.0 / math.sqrt(2.0 * math.pi))


def dot(a, b, dims):
    return lax.dot_general(a, b, (dims, ((), ())), preferred_element_type=F32)


NN = ((1,), (0,))
NT = ((1,), (1,))
TN = ((0,), (0,))


def line_gather(shard, z, n):
    up = [shard]
    down = [shard]
    for s in range(1, n):
        up.append(lax.ppermute(up[-1], "outer", [(i, i + 1) for i in range(s - 1, n - 1)]))
        down.append(lax.ppermute(down[-1], "outer", [(i, i - 1) for i in range(1, n - s + 1)]))
    slots = [shard] + [jnp.where(z >= k, up[k], down[n - k]) for k in range(1, n)]
    return jnp.concatenate(slots, axis=0)


def line_scatter(full, n):
    rows = full.shape[0] // n
    part = [lax.slice_in_dim(full, k * rows, (k + 1) * rows) for k in range(n)]
    up = down = None
    for s in range(1, n):
        a = part[s] if up is None else part[s] + up.astype(F32)
        b = part[n - s] if down is None else part[n - s] + down.astype(F32)
        up = lax.ppermute(a.astype(BF16), "outer", [(i, i + 1) for i in range(0, s)])
        down = lax.ppermute(b.astype(BF16), "outer", [(i, i - 1) for i in range(n - s, n)])
    return part[0] + up.astype(F32) + down.astype(F32)


def local(
    tokens, lengths, w_qkv, b_qkv, w_out, b_out, w_fc, b_fc, w_proj, b_proj,
    gain_attn, shift_attn, gain_mlp, shift_mlp, cotangent,
):
    n = lax.axis_size("outer")
    z = lax.axis_index("outer")
    inner = lax.axis_index("inner")
    tensor = lax.axis_index("tensor")
    n_tensor = lax.axis_size("tensor")
    own_rows, width = tokens.shape
    group_rows = own_rows * n_tensor
    block = width // n
    heads = w_qkv.shape[1]
    per = heads // INNER
    ff = w_fc.shape[1] // INNER
    wide = ff // CHUNKS

    def turn(v):
        parts = v.reshape(v.shape[:-1] + (n, block))
        return jnp.concatenate(
            [lax.dynamic_index_in_dim(parts, lax.rem(z - k + n, n), v.ndim - 1, False) for k in range(n)],
            axis=-1,
        )

    def spread_cols(w, pieces):
        rows = w.shape[0]
        w = w.reshape(rows, INNER, -1)
        return lax.all_to_all(w, "inner", 1, 0, tiled=False).reshape(INNER * rows, -1)

    lens = lax.all_gather(lengths, "inner", axis=0, tiled=True)
    x_turned = turn(tokens)
    own_index = tensor * own_rows + jnp.arange(own_rows, dtype=jnp.int32)
    own_live = (layout(lengths[0], own_index)[0] < 2).astype(F32)[:, None]
    cot_float = cotangent.astype(F32)
    grad_own = cot_float * own_live
    x_all = lax.all_gather(x_turned, ("inner", "tensor"), axis=0, tiled=True)
    grad_branch = lax.all_gather(turn(grad_own.astype(BF16)), ("inner", "tensor"), axis=0, tiled=True)

    fc_rows = spread_cols(w_fc, 1)
    proj_rows = spread_cols(w_proj, 1)
    qkv_rows = spread_cols(w_qkv.reshape(w_qkv.shape[0], -1), 1)
    out_rows = spread_cols(w_out.reshape(w_out.shape[0], -1), 1)

    def gather_mlp(c):
        cols = slice(c * wide, (c + 1) * wide)
        return line_gather(fc_rows[:, cols], z, n), line_gather(proj_rows[:, cols], z, n)

    ga, sa, gm, sm = turn(gain_attn), turn(shift_attn), turn(gain_mlp), turn(shift_mlp)
    xhat, _ = norm_stats(x_all.astype(F32))
    normed_attn = (xhat * ga + sa).astype(BF16)
    normed_mlp = (xhat * gm + sm).astype(BF16)
    b_fc_own = lax.dynamic_slice_in_dim(b_fc, inner * ff, ff)
    b_qkv_own = lax.dynamic_slice_in_dim(b_qkv, inner * per, per).reshape(-1)

    hidden_all, pre_all, fc_all, proj_all = [], [], [], []
    sum_fc, sum_proj, bias_fc = [], [], []

    def mlp(c):
        fc, proj = gather_mlp(c)
        hidden_pre = dot(normed_mlp, fc, NN) + b_fc_own[c * wide : (c + 1) * wide]
        hidden = jax.nn.gelu(hidden_pre, approximate=False).astype(BF16)
        sum_proj.append(line_scatter(dot(grad_branch, hidden, TN), n))
        grad_pre = (dot(grad_branch, proj, NN) * gelu_slope(hidden_pre)).astype(BF16)
        sum_fc.append(line_scatter(dot(normed_mlp, grad_pre, TN), n))
        bias_fc.append(jnp.sum(grad_pre.astype(F32), axis=0))
        hidden_all.append(hidden)
        pre_all.append(grad_pre)
        fc_all.append(fc)
        proj_all.append(proj)

    mlp(0)

    qkv = line_gather(qkv_rows, z, n)
    out = line_gather(out_rows, z, n)
    t_all = x_all.shape[0]
    groups = t_all // group_rows
    row_index = jnp.arange(group_rows, dtype=jnp.int32)
    segment, position = jax.vmap(lambda l: layout(l, row_index))(lens)
    cosine, sine_part = angles(position)
    cosine, sine_part = cosine[:, :, None], sine_part[:, :, None]
    joined = (dot(normed_attn, qkv, NN) + b_qkv_own).reshape(groups, group_rows, per, 3 * HEAD)
    queries = rotary(joined[..., :HEAD], cosine, sine_part).astype(BF16)
    key_rot = rotary(joined[..., HEAD : 2 * HEAD], cosine, sine_part).astype(BF16)
    values = joined[..., 2 * HEAD :].astype(BF16)
    scale = 1.0 / math.sqrt(HEAD)
    scores = jnp.einsum("gqhe,gkhe->ghqk", queries, key_rot, preferred_element_type=F32) * scale
    allowed = (segment[:, :, None] == segment[:, None, :]) & (row_index[:, None] >= row_index[None, :])
    scores = jnp.where(allowed[:, None], scores, -1e30)
    shifted = jnp.exp(scores - jnp.max(scores, axis=-1, keepdims=True))
    probs = shifted / jnp.sum(shifted, axis=-1, keepdims=True)
    probs_low = probs.astype(BF16)
    mixed = jnp.einsum("ghqk,gkhe->gqhe", probs_low, values, preferred_element_type=F32).astype(BF16)
    mixed_flat = mixed.reshape(t_all, per * HEAD)
    sum_out = line_scatter(dot(grad_branch, mixed_flat, TN), n)
    grad_mixed = dot(grad_branch, out, NN).astype(BF16).reshape(groups, group_rows, per, HEAD)
    grad_probs = jnp.einsum("gqhe,gkhe->ghqk", grad_mixed, values, preferred_element_type=F32)
    grad_scores = (
        probs * (grad_probs - jnp.sum(probs * grad_probs, axis=-1, keepdims=True))
    ).astype(BF16)
    grad_values = jnp.einsum("ghqk,gqhe->gkhe", probs_low, grad_mixed, preferred_element_type=F32)
    grad_queries = jnp.einsum("ghqk,gkhe->gqhe", grad_scores, key_rot, preferred_element_type=F32) * scale
    grad_keys = jnp.einsum("ghqk,gqhe->gkhe", grad_scores, queries, preferred_element_type=F32) * scale
    grad_joined = jnp.concatenate(
        [rotary(grad_queries, cosine, -sine_part), rotary(grad_keys, cosine, -sine_part), grad_values],
        axis=-1,
    ).astype(BF16).reshape(t_all, per * 3 * HEAD)
    sum_qkv = line_scatter(dot(normed_attn, grad_joined, TN), n)
    bias_qkv = jnp.sum(grad_joined.astype(F32), axis=0)

    for c in range(1, CHUNKS):
        mlp(c)

    left = jnp.concatenate(hidden_all + [mixed_flat], axis=1)
    right = jnp.concatenate(proj_all + [out], axis=1)
    branch = dot(left, right, NT).astype(BF16)
    branch_own = lax.psum_scatter(branch, ("inner", "tensor"), scatter_dimension=0, tiled=True)
    n_attn = dot(grad_joined, qkv, NT)
    n_mlp = dot(jnp.concatenate(pre_all, axis=1), jnp.concatenate(fc_all, axis=1), NT)
    u = (n_attn * ga + n_mlp * gm).astype(BF16)
    u_own = lax.psum_scatter(u, ("inner", "tensor"), scatter_dimension=0, tiled=True).astype(F32)

    def back(v):
        parts = v.reshape(v.shape[:-1] + (n, block))
        return jnp.concatenate(
            [lax.dynamic_index_in_dim(parts, lax.rem(z - k + n, n), v.ndim - 1, False) for k in range(n)],
            axis=-1,
        )

    residual = tokens.astype(F32)
    own_hat, own_inv = norm_stats(residual)
    output = residual + own_live * (back(branch_own).astype(F32) + b_out + b_proj)
    u_back = back(u_own)
    grad_tokens = cot_float + own_inv * (
        u_back
        - jnp.mean(u_back, axis=-1, keepdims=True)
        - own_hat * jnp.mean(u_back * own_hat, axis=-1, keepdims=True)
    )

    cols = jnp.stack(
        [
            jnp.sum(n_attn * xhat, axis=0),
            jnp.sum(n_attn, axis=0),
            jnp.sum(n_mlp * xhat, axis=0),
            jnp.sum(n_mlp, axis=0),
        ]
    )
    cols = jnp.concatenate([jnp.sum(grad_own, axis=0)[None], back(cols)], axis=0)
    place = tensor * INNER + inner
    full_qkv = jnp.zeros((n_tensor * INNER, per * 3 * HEAD), F32)
    full_qkv = lax.dynamic_update_index_in_dim(full_qkv, bias_qkv, place, 0)
    full_fc = jnp.zeros((n_tensor * INNER, ff), F32)
    full_fc = lax.dynamic_update_index_in_dim(full_fc, jnp.concatenate(bias_fc), place, 0)
    flat = lax.psum(
        jnp.concatenate([cols.reshape(-1), full_qkv.reshape(-1), full_fc.reshape(-1)]),
        ("outer", "inner", "tensor"),
    )
    cols = flat[: 5 * width].reshape(5, width)
    g_qkv = flat[5 * width : 5 * width + full_qkv.size].reshape(n_tensor, heads, 3 * HEAD)
    g_fc = flat[5 * width + full_qkv.size :].reshape(n_tensor, INNER * ff)

    def collect(own):
        rows = own.shape[0] // INNER
        got = lax.all_to_all(own.astype(BF16).reshape(INNER, rows, -1), "inner", 0, 1, tiled=False)
        return got.reshape(rows, -1).astype(F32)

    return (
        output.astype(BF16),
        grad_tokens.astype(BF16),
        collect(sum_qkv).reshape(w_qkv.shape),
        lax.dynamic_index_in_dim(g_qkv, tensor, 0, False),
        collect(sum_out).reshape(w_out.shape),
        cols[0],
        collect(jnp.concatenate(sum_fc, axis=1)),
        lax.dynamic_index_in_dim(g_fc, tensor, 0, False),
        collect(jnp.concatenate(sum_proj, axis=1)),
        cols[0],
        cols[1],
        cols[2],
        cols[3],
        cols[4],
    )


def solution(mesh):
    n_dp, n_tensor = mesh.devices.shape
    split = Mesh(
        mesh.devices.reshape(n_dp // INNER, INNER, n_tensor), ("outer", "inner", "tensor")
    )
    dp = ("outer", "inner")
    rows = P(("outer", "inner", "tensor"), None)
    w3 = P(dp, "tensor", None)
    w2 = P(dp, "tensor")
    return jax.shard_map(
        local,
        mesh=split,
        in_specs=(
            rows, P(dp, None), w3, P("tensor", None), w3, P(), w2, P("tensor"), w2, P(),
            P(), P(), P(), P(), rows,
        ),
        out_specs=(
            rows, rows, w3, P("tensor", None), w3, P(), w2, P("tensor"), w2, P(), P(), P(), P(), P(),
        ),
        check_vma=False,
    )
```

time: 1740 us -> 1170 us (0.67)
  waiting for transfers between devices: 1380 us -> 364 us
  starting transfers between devices: 1.27 us -> 349 us
  other arithmetic: 28.1 us -> 142 us
  blocking collectives: 99.2 us -> 6.92 us
  local copies, waits for them, and re-layouts: 26.5 us -> 77.8 us
    reduce_scatter x7 -> x2, waiting for transfers between devices: 977 us -> 73.2 us  [the longest x1 73.2 us: local(): lax.psum_scatter(branch, ('inner', 'tensor'), scatter_dimension=0, tiled=...]
    all_gather x7 -> x2, waiting for transfers between devices: 400 us -> 21.3 us  [the longest x1 21.3 us: local(): lax.all_gather(turn(grad_own.astype(BF16)), ('inner', 'tensor'), axis=0,...]
    ppermute x0 -> x120, starting transfers between devices: none -> 318 us  [the longest x30 162 us: line_scatter(): lax.ppermute(a.astype(BF16), 'outer', [(i, i + 1) for i in range(0, s)])]
    ppermute x0 -> x120, waiting for transfers between devices: none -> 144 us  [the longest x30 88.4 us: line_gather(): lax.ppermute(down[-1], 'outer', [(i, i - 1) for i in range(1, n - s + 1)])]
    psum x0 -> x1, waiting for transfers between devices: none -> 108 us  [local(): lax.psum(jnp.concatenate([cols.reshape(-1), full_qkv.reshape(-1), full_fc...]
    psum x2 -> x0, blocking collectives: 99.2 us -> none  [the longest x1 58.3 us: local(): bias_qkv, bias_fc = lax.psum((grad_bias_qkv, grad_bias_fc), 'dp')]
    convert_element_type x5 -> x41, other arithmetic: 10.3 us -> 48.1 us  [the longest x20 21.1 us: line_scatter(): a.astype(BF16)]
    reduce_sum x5 -> x9, other arithmetic: 11.6 us -> 41.8 us  [the longest x1 28.4 us: local(): jnp.sum(n_mlp, axis=0)]
  transfers between devices with their start and end apart: 14 -> 133, of which waited for: 11 -> 38; matrix products, arithmetic and copies ran while one was open for 13% -> 19% of each run, Pallas kernels for 0% -> 0%
where the time goes in v1:
time: 1170 us; the launch traced here: 1150 us
  waiting for transfers between devices  364 us (31%)
  starting transfers between devices  349 us (30%)
  matrix products  196 us (17%)
  other arithmetic  142 us (12%)
  local copies, waits for them, and re-layouts  77.8 us (7%)
  between operations  19.8 us (2%)
    dot_general x23, matrix products, dot(): return lax.dot_general(a, b, (dims, ((), ())), preferred_element_type=F32)  180 us
    ppermute x30, starting transfers between devices, line_scatter(): lax.ppermute(a.astype(BF16), 'outer', [(i, i + 1) for i in range(0, s)])  162 us
    psum x1, waiting for transfers between devices, local(): lax.psum(jnp.concatenate([cols.reshape(-1), full_qkv.reshape(-1), full_fc...  108 us
    ppermute x30, waiting for transfers between devices, line_gather(): lax.ppermute(down[-1], 'outer', [(i, i - 1) for i in range(1, n - s + 1)])  88.4 us
    ppermute x30, starting transfers between devices, line_gather(): lax.ppermute(up[-1], 'outer', [(i, i + 1) for i in range(s - 1, n - 1)])  75.5 us
    reduce_scatter x1, waiting for transfers between devices, local(): lax.psum_scatter(branch, ('inner', 'tensor'), scatter_dimension=0, tiled=...  73.2 us
    ppermute x30, starting transfers between devices, line_gather(): lax.ppermute(down[-1], 'outer', [(i, i - 1) for i in range(1, n - s + 1)])  51 us
    ppermute x30, waiting for transfers between devices, line_scatter(): lax.ppermute(a.astype(BF16), 'outer', [(i, i + 1) for i in range(0, s)])  47.9 us
  transfers between devices with their start and end apart: 133, of which 38 were waited for; matrix products, arithmetic and copies ran while one was open for 19% of the time, Pallas kernels for 0%

profile of v1, /device:TPU:0, one launch (start us, length us, event | category | flops | bytes accessed | tf_op | source)
XLA Modules:
  0.0 1154.8 jit_solution(4720249424705469222)
XLA Ops:
  17.7 6.9 all-gather
  113.9 9.2 collective-permute-start.42
  145.7 7.6 collective-permute-start.48
  170.7 7.9 collective-permute-start.24
  180.4 9.4 collective-permute-done.50
  222.0 8.0 collective-permute-done.39
  233.2 6.8 collective-permute-done.45
  240.8 13.3 %collective-permute-start.51 = (bf16[512,256]{1,0:T(8,128)(2,1)S(1)}, bf16[512,256]{1,0:T(8,128)(2,1)S(1)}, u32[]{:S(2)}, u32[]{:S(2)}) collective-permute-start(bf16[512,256]{1,0:T(8,128)(2,1)S(1)} %collective-permute-done.50), channel_id=1, source_target_pairs={{8,0},{9,1},{10,2},{11,3},{12,4},{13,5},{14,6},{15,7}} | collective-permute-start | bytes 786440 | tf_op jit(solution)/shard_map/ppermute | solution.py:73
  260.5 10.1 collective-permute-done.26
  272.9 18.7 %collective-permute-done.27 = bf16[512,768]{1,0:T(8,128)(2,1)S(1)} collective-permute-done((bf16[512,768]{1,0:T(8,128)(2,1)S(1)}, bf16[512,768]{1,0:T(8,128)(2,1)S(1)}, u32[]{:S(2)}, u32[]{:S(2)}) %collective-permute-start.27) | collective-permute-done | bytes 786464 | tf_op jit(solution)/shard_map/ppermute | solution.py:73
  300.2 7.9 fusion.10
  308.1 8.7 broadcast_add_fusion
  337.8 12.1 %constant_dynamic-update-slice_fusion.4 = (bf16[2048,1280]{0,1:T(8,128)(2,1)S(1)}, bf16[2048,256]{0,1:T(8,128)(2,1)}, f32[2048,256]{0,1:T(8,128)}) fusion(f32[256]{0:T(256)S(1)} %get-tuple-element.177, bf16[2048,2048]{1,0:T(8,128)(2,1)S(1)} %bitcast.276, bf16[512,256]{1,0:T(8,128)(2,1)S(1)} %copy-done.48, ...), kind=kOutput, calls=%fused_computation.451 | convolution fusion | flops 2186280960 | bytes 13632512 | tf_op jit(solution)/shard_map/dot_general | solution.py:60
  350.0 12.1 %constant_dynamic-update-slice_fusion.3 = (bf16[2048,1280]{0,1:T(8,128)(2,1)S(1)}, bf16[2048,256]{0,1:T(8,128)(2,1)}, f32[2048,256]{0,1:T(8,128)}) fusion(bf16[2048,1280]{0,1:T(8,128)(2,1)S(1)} %get-tuple-element.60, f32[256]{0:T(256)S(1)} %get-tuple-element.176, bf16[2048,2048]{1,0:T(8,128)(2,1)S(1)} %bitcast.276, bf16[512,256]{1,0:T(8,128)(2,1)S(1)} %copy-done.52, ...), kind=kOutput, calls=%fused_computation.450 | convolution fusion | flops 2186280960 | bytes 13632512 | tf_op jit(solution)/shard_map/dot_general | solution.py:60
  362.1 12.3 %constant_dynamic-update-slice_fusion.2 = (bf16[2048,1280]{0,1:T(8,128)(2,1)S(1)}, bf16[2048,256]{0,1:T(8,128)(2,1)}, f32[2048,256]{0,1:T(8,128)}) fusion(bf16[2048,1280]{0,1:T(8,128)(2,1)S(1)} %get-tuple-element.58, f32[256]{0:T(256)S(1)} %get-tuple-element.175, bf16[2048,2048]{1,0:T(8,128)(2,1)S(1)} %bitcast.276, bf16[512,256]{1,0:T(8,128)(2,1)S(1)} %copy-done.58, ...), kind=kOutput, calls=%fused_computation.449 | convolution fusion | flops 2186280960 | bytes 13632512 | tf_op jit(solution)/shard_map/dot_general | solution.py:60
  374.4 11.2 constant_dynamic-update-slice_fusion.1
  385.8 13.2 %convolution_convert_fusion = bf16[2048,2048]{1,0:T(8,128)(2,1)} fusion(bf16[2048,1280]{0,1:T(8,128)(2,1)S(1)} %constant_dynamic-update-slice_fusion, bf16[2048,1280]{1,0:T(8,128)(2,1)S(1)} %bitcast.326), kind=kOutput, calls=%fused_computation.17 | convolution fusion | flops 10741612544 | bytes 18874368 | tf_op jit(solution)/shard_map/dot_general | solution.py:60
  403.9 73.2 %reduce-scatter.3.cloned.1.call-done = bf16[256,2048]{1,0:T(8,128)(2,1)} async-done(((bf16[2048,2048]{1,0:T(8,128)(2,1)}), bf16[256,2048]{1,0:T(8,128)(2,1)}) %reduce-scatter.3.cloned.1.call-update) | async-done | bytes 1048592 | tf_op jit(solution)/shard_map/reduce_scatter | solution.py:205
  487.3 28.4 %fusion.22.clone.5 = bf16[2048,1024]{1,0:T(8,128)(2,1)} fusion(bf16[512,256]{1,0:T(8,128)(2,1)S(1)} %copy-done.63, bf16[512,256]{1,0:T(8,128)(2,1)S(1)} %copy-done.47, bf16[512,256]{1,0:T(8,128)(2,1)S(1)} %copy-done.61, bf16[512,256]{1,0:T(8,128)(2,1)S(1)} %copy-done.67, bf16[512,256]{1,0:T(8,128)(2,1)S(1)} %copy-done.59, ...), kind=kLoop, calls=%fused_computation.27.clone.clone.clone.2 | loop fusion | flops 67108864 | bytes 8388608 | tf_op jit(solution)/shard_map/reduce_sum | solution.py:233
  518.7 21.3 %all-gather.6.cloned.1.call-done = bf16[2048,2048]{1,0:T(8,128)(2,1)} async-done(((bf16[256,2048]{1,0:T(8,128)(2,1)}), bf16[2048,2048]{1,0:T(8,128)(2,1)}) %all-gather.6.cloned.1.call-update) | async-done | bytes 8388624 | tf_op jit(solution)/shard_map/all_gather | solution.py:126
  554.5 6.9 fusion.159
  569.8 12.1 %fusion.199 = f32[2048,2048]{1,0:T(8,128)} fusion(bf16[2048,768]{1,0:T(8,128)(2,1)S(1)} %concatenate.200, bf16[512,768]{1,0:T(8,128)(2,1)} %copy-done.116, bf16[512,768]{1,0:T(8,128)(2,1)} %copy-done.115, bf16[512,768]{1,0:T(8,128)(2,1)} %copy-done.117, bf16[512,768]{1,0:T(8,128)(2,1)} %bitcast.32), kind=kOutput, calls=%fused_computation.307 | convolution fusion | flops 6455033856 | bytes 23068672 | tf_op jit(solution)/shard_map/dot_general | solution.py:60
  582.4 11.2 fusion.271
  620.8 8.2 convert_reduce_fusion.6
  634.0 7.6 convert_reduce_fusion.5
  646.5 7.8 convert_reduce_fusion.4
  673.2 20.0 %fusion.245 = (f32[2048]{0:T(1024)S(1)}, f32[2048]{0:T(1024)S(1)}, bf16[2048,2048]{1,0:T(8,128)(2,1)}, f32[2048]{0:T(1024)S(1)}, f32[2048]{0:T(1024)S(1)}) fusion(f32[2048]{0:T(1024)S(1)} %copy-done.178, f32[2048]{0:T(1024)S(1)} %copy-done.176, bf16[2048,2048]{1,0:T(8,128)(2,1)S(1)} %bitcast.273, f32[2048]{0:T(1024)} %pad_maximum_fusion.21, ...), kind=kOutput, calls=%fused_computation.537 | convolution fusion | flops 8661229568 | bytes 42008576 | tf_op jit(solution)/shard_map/dot_general | solution.py:60
  705.8 107.7 %all-reduce.2.cloned.1.call-done = f32[24576]{0:T(1024)} async-done(((f32[24576]{0:T(1024)}), f32[24576]{0:T(1024)}) %all-reduce.2.cloned.1.call-update) | async-done | bytes 98320 | tf_op jit(solution)/shard_map/psum | solution.py:242
  916.1 15.2 %collective-permute-done.85 = bf16[512,256]{1,0:T(8,128)(2,1)S(1)} collective-permute-done((bf16[512,256]{1,0:T(8,128)(2,1)S(1)}, bf16[512,256]{1,0:T(8,128)(2,1)S(1)}, u32[]{:S(2)}, u32[]{:S(2)}) %collective-permute-start.85) | collective-permute-done | bytes 262176 | tf_op jit(solution)/shard_map/ppermute | solution.py:85
  958.7 30.7 %collective-permute-start.68 = (bf16[512,256]{1,0:T(8,128)(2,1)S(1)}, bf16[512,256]{1,0:T(8,128)(2,1)S(1)}, u32[]{:S(2)}, u32[]{:S(2)}) collective-permute-start(bf16[512,256]{1,0:T(8,128)(2,1)S(1)} %get-tuple-element.113), channel_id=1, source_target_pairs={{0,8},{8,16},{16,24},{1,9},{9,17},{17,25},{2,10},{10,18},{18,26},{... | collective-permute-start | bytes 786440 | tf_op jit(solution)/shard_map/ppermute | solution.py:85
  1026.6 9.6 collective-permute-done.116
  1074.4 17.7 %collective-permute-start.62 = (bf16[512,768]{1,0:T(8,128)(2,1)}, bf16[512,768]{1,0:T(8,128)(2,1)}, u32[]{:S(2)}, u32[]{:S(2)}) collective-permute-start(bf16[512,768]{1,0:T(8,128)(2,1)} %get-tuple-element.71), channel_id=1, source_target_pairs={{0,8},{8,16},{16,24},{1,9},{9,17},{17,25},{2,10},{10,18},{18,26},{... | collective-permute-start | bytes 2359304 | tf_op jit(solution)/shard_map/ppermute | solution.py:85
  (918 shorter events, 582.1 us)
Async XLA Ops:
  7.2 284.6 %all-gather.4.cloned.1.call-start = ((), (), s32[]{:S(2)}) async-start(), calls=%async_computation.10 | async-start | bytes 9437184 | tf_op jit(solution)/shard_map/all_gather | solution.py:125
  78.0 81.0 %all-to-all-start.1 = ((bf16[1,128,4,768]{3,1,0,2:T(8,128)(2,1)}), bf16[1,128,4,768]{3,1,0,2:T(8,128)(2,1)}, u32[]{:S(2)}, u32[]{:S(2)}) async-start(bf16[1,128,4,768]{3,1,0,2:T(8,128)(2,1)} %bitcast.249), calls=%async_computation.1 | async-start | bytes 1572864 | tf_op jit(solution)/shard_map/all_to_all | solution.py:117
  82.2 394.8 %reduce-scatter.3.cloned.1.call-start = ((), (), s32[]{:S(2)}) async-start(), calls=%async_computation.11 | async-start | bytes 9437184 | tf_op jit(solution)/shard_map/reduce_scatter | solution.py:205
  159.1 96.2 %collective-permute-start.25 = (bf16[512,768]{1,0:T(8,128)(2,1)}, bf16[512,768]{1,0:T(8,128)(2,1)S(1)}, u32[]{:S(2)}, u32[]{:S(2)}) collective-permute-start(bf16[512,768]{1,0:T(8,128)(2,1)} %bitcast.32), channel_id=1, source_target_pairs={{8,0},{16,8},{24,16},{9,1},{17,9},{25,17},{10,2},{18,10},{26,18},{... | collective-permute-start | bytes 2359304 | tf_op jit(solution)/shard_map/ppermute | solution.py:73
  170.7 85.4 %collective-permute-start.24 = (bf16[512,768]{1,0:T(8,128)(2,1)}, bf16[512,768]{1,0:T(8,128)(2,1)S(1)}, u32[]{:S(2)}, u32[]{:S(2)}) collective-permute-start(bf16[512,768]{1,0:T(8,128)(2,1)} %bitcast.32), channel_id=1, source_target_pairs={{0,8},{8,16},{16,24},{1,9},{9,17},{17,25},{2,10},{10,18},{18,26},{... | collective-permute-start | bytes 2359304 | tf_op jit(solution)/shard_map/ppermute | solution.py:72
  205.7 53.9 %collective-permute-start.21 = (bf16[512,256]{1,0:T(8,128)(2,1)S(1)}, bf16[512,256]{1,0:T(8,128)(2,1)S(1)}, u32[]{:S(2)}, u32[]{:S(2)}) collective-permute-start(bf16[512,256]{1,0:T(8,128)(2,1)S(1)} %copy-done.143), channel_id=1, source_target_pairs={{8,0},{9,1},{10,2},{11,3},{12,4},{13,5},{14,6},{15,7}} | collective-permute-start | bytes 786440 | tf_op jit(solution)/shard_map/ppermute | solution.py:73
  231.3 40.6 %collective-permute-start.23 = (bf16[512,256]{1,0:T(8,128)(2,1)S(1)}, bf16[512,256]{1,0:T(8,128)(2,1)S(1)}, u32[]{:S(2)}, u32[]{:S(2)}) collective-permute-start(bf16[512,256]{1,0:T(8,128)(2,1)S(1)} %copy-done.138), channel_id=1, source_target_pairs={{16,24},{17,25},{18,26},{19,27},{20,28},{21,29},{22,30},{23,31}} | collective-permute-start | bytes 786440 | tf_op jit(solution)/shard_map/ppermute | solution.py:72
  399.0 141.0 %all-gather.6.cloned.1.call-start = ((), (), s32[]{:S(2)}) async-start(), calls=%async_computation.12 | async-start | bytes 9437184 | tf_op jit(solution)/shard_map/all_gather | solution.py:126
  485.4 328.0 %all-reduce.2.cloned.1.call-start = ((), (), s32[]{:S(2)}) async-start(), calls=%async_computation.14 | async-start | bytes 196608 | tf_op jit(solution)/shard_map/psum | solution.py:242
  597.2 217.7 %collective-permute-start.96 = (bf16[512,256]{1,0:T(8,128)(2,1)}, bf16[512,256]{1,0:T(8,128)(2,1)}, u32[]{:S(2)}, u32[]{:S(2)}) collective-permute-start(bf16[512,256]{1,0:T(8,128)(2,1)} %get-tuple-element.83), channel_id=1, source_target_pairs={{0,8},{1,9},{2,10},{3,11},{4,12},{5,13},{6,14},{7,15}} | collective-permute-start | bytes 786440 | tf_op jit(solution)/shard_map/ppermute | solution.py:85
  601.3 257.5 %collective-permute-start.99 = (bf16[512,256]{1,0:T(8,128)(2,1)}, bf16[512,256]{1,0:T(8,128)(2,1)}, u32[]{:S(2)}, u32[]{:S(2)}) collective-permute-start(bf16[512,256]{1,0:T(8,128)(2,1)} %get-tuple-element.84), channel_id=1, source_target_pairs={{24,16},{25,17},{26,18},{27,19},{28,20},{29,21},{30,22},{31,23}} | collective-permute-start | bytes 786440 | tf_op jit(solution)/shard_map/ppermute | solution.py:86
  606.5 210.4 %collective-permute-start.102 = (bf16[512,256]{1,0:T(8,128)(2,1)}, bf16[512,256]{1,0:T(8,128)(2,1)}, u32[]{:S(2)}, u32[]{:S(2)}) collective-permute-start(bf16[512,256]{1,0:T(8,128)(2,1)} %get-tuple-element.87), channel_id=1, source_target_pairs={{0,8},{1,9},{2,10},{3,11},{4,12},{5,13},{6,14},{7,15}} | collective-permute-start | bytes 786440 | tf_op jit(solution)/shard_map/ppermute | solution.py:85
  608.5 257.7 %collective-permute-start.105 = (bf16[512,256]{1,0:T(8,128)(2,1)}, bf16[512,256]{1,0:T(8,128)(2,1)}, u32[]{:S(2)}, u32[]{:S(2)}) collective-permute-start(bf16[512,256]{1,0:T(8,128)(2,1)} %get-tuple-element.88), channel_id=1, source_target_pairs={{24,16},{25,17},{26,18},{27,19},{28,20},{29,21},{30,22},{31,23}} | collective-permute-start | bytes 786440 | tf_op jit(solution)/shard_map/ppermute | solution.py:86
  613.5 209.9 %collective-permute-start.108 = (bf16[512,256]{1,0:T(8,128)(2,1)}, bf16[512,256]{1,0:T(8,128)(2,1)}, u32[]{:S(2)}, u32[]{:S(2)}) collective-permute-start(bf16[512,256]{1,0:T(8,128)(2,1)} %get-tuple-element.91), channel_id=1, source_target_pairs={{0,8},{1,9},{2,10},{3,11},{4,12},{5,13},{6,14},{7,15}} | collective-permute-start | bytes 786440 | tf_op jit(solution)/shard_map/ppermute | solution.py:85
  694.4 442.3 %reduce-scatter.5.cloned.1.call-start = ((), (), s32[]{:S(2)}) async-start(), calls=%async_computation.13 | async-start | bytes 9437184 | tf_op jit(solution)/shard_map/reduce_scatter | solution.py:209
  814.9 59.5 %collective-permute-start.111 = (bf16[512,256]{1,0:T(8,128)(2,1)}, bf16[512,256]{1,0:T(8,128)(2,1)S(1)}, u32[]{:S(2)}, u32[]{:S(2)}) collective-permute-start(bf16[512,256]{1,0:T(8,128)(2,1)} %get-tuple-element.92), channel_id=1, source_target_pairs={{24,16},{25,17},{26,18},{27,19},{28,20},{29,21},{30,22},{31,23}} | collective-permute-start | bytes 786440 | tf_op jit(solution)/shard_map/ppermute | solution.py:86
  858.8 33.3 %collective-permute-start.75 = (bf16[512,256]{1,0:T(8,128)(2,1)S(1)}, bf16[512,256]{1,0:T(8,128)(2,1)S(1)}, u32[]{:S(2)}, u32[]{:S(2)}) collective-permute-start(bf16[512,256]{1,0:T(8,128)(2,1)S(1)} %copy-done.130), channel_id=1, source_target_pairs={{24,16},{25,17},{26,18},{27,19},{28,20},{29,21},{30,22},{31,23}} | collective-permute-start | bytes 786440 | tf_op jit(solution)/shard_map/ppermute | solution.py:86
  866.1 36.8 %collective-permute-start.81 = (bf16[512,256]{1,0:T(8,128)(2,1)S(1)}, bf16[512,256]{1,0:T(8,128)(2,1)S(1)}, u32[]{:S(2)}, u32[]{:S(2)}) collective-permute-start(bf16[512,256]{1,0:T(8,128)(2,1)S(1)} %copy-done.129), channel_id=1, source_target_pairs={{24,16},{25,17},{26,18},{27,19},{28,20},{29,21},{30,22},{31,23}} | collective-permute-start | bytes 786440 | tf_op jit(solution)/shard_map/ppermute | solution.py:86
  874.4 39.7 %collective-permute-start.87 = (bf16[512,256]{1,0:T(8,128)(2,1)S(1)}, bf16[512,256]{1,0:T(8,128)(2,1)S(1)}, u32[]{:S(2)}, u32[]{:S(2)}) collective-permute-start(bf16[512,256]{1,0:T(8,128)(2,1)S(1)} %copy-done.128), channel_id=1, source_target_pairs={{24,16},{25,17},{26,18},{27,19},{28,20},{29,21},{30,22},{31,23}} | collective-permute-start | bytes 786440 | tf_op jit(solution)/shard_map/ppermute | solution.py:86
  882.4 54.2 %collective-permute-start.93 = (bf16[512,256]{1,0:T(8,128)(2,1)S(1)}, bf16[512,256]{1,0:T(8,128)(2,1)S(1)}, u32[]{:S(2)}, u32[]{:S(2)}) collective-permute-start(bf16[512,256]{1,0:T(8,128)(2,1)S(1)} %get-tuple-element.112), channel_id=1, source_target_pairs={{24,16},{25,17},{26,18},{27,19},{28,20},{29,21},{30,22},{31,23}} | collective-permute-start | bytes 786440 | tf_op jit(solution)/shard_map/ppermute | solution.py:86
  892.1 50.0 %collective-permute-start.69 = (bf16[512,256]{1,0:T(8,128)(2,1)S(1)}, bf16[512,256]{1,0:T(8,128)(2,1)S(1)}, u32[]{:S(2)}, u32[]{:S(2)}) collective-permute-start(bf16[512,256]{1,0:T(8,128)(2,1)S(1)} %copy-done.146), channel_id=1, source_target_pairs={{24,16},{25,17},{26,18},{27,19},{28,20},{29,21},{30,22},{31,23}} | collective-permute-start | bytes 786440 | tf_op jit(solution)/shard_map/ppermute | solution.py:86
  903.0 43.7 %collective-permute-start.60 = (bf16[512,768]{1,0:T(8,128)(2,1)S(1)}, bf16[512,768]{1,0:T(8,128)(2,1)S(1)}, u32[]{:S(2)}, u32[]{:S(2)}) collective-permute-start(bf16[512,768]{1,0:T(8,128)(2,1)S(1)} %copy-done.119), channel_id=1, source_target_pairs={{0,8},{1,9},{2,10},{3,11},{4,12},{5,13},{6,14},{7,15}} | collective-permute-start | bytes 2359304 | tf_op jit(solution)/shard_map/ppermute | solution.py:85
  937.2 67.1 %collective-permute-start.98 = (bf16[512,256]{1,0:T(8,128)(2,1)}, bf16[512,256]{1,0:T(8,128)(2,1)S(1)}, u32[]{:S(2)}, u32[]{:S(2)}) collective-permute-start(bf16[512,256]{1,0:T(8,128)(2,1)} %get-tuple-element.81), channel_id=1, source_target_pairs={{0,8},{8,16},{16,24},{1,9},{9,17},{17,25},{2,10},{10,18},{18,26},{... | collective-permute-start | bytes 786440 | tf_op jit(solution)/shard_map/ppermute | solution.py:85
  942.8 62.4 %collective-permute-start.104 = (bf16[512,256]{1,0:T(8,128)(2,1)}, bf16[512,256]{1,0:T(8,128)(2,1)S(1)}, u32[]{:S(2)}, u32[]{:S(2)}) collective-permute-start(bf16[512,256]{1,0:T(8,128)(2,1)} %get-tuple-element.85), channel_id=1, source_target_pairs={{0,8},{8,16},{16,24},{1,9},{9,17},{17,25},{2,10},{10,18},{18,26},{... | collective-permute-start | bytes 786440 | tf_op jit(solution)/shard_map/ppermute | solution.py:85
  954.4 35.1 %collective-permute-start.88 = (bf16[512,256]{1,0:T(8,128)(2,1)S(1)}, bf16[512,256]{1,0:T(8,128)(2,1)S(1)}, u32[]{:S(2)}, u32[]{:S(2)}) collective-permute-start(bf16[512,256]{1,0:T(8,128)(2,1)S(1)} %get-tuple-element.106), channel_id=1, source_target_pairs={{16,8},{24,16},{17,9},{25,17},{18,10},{26,18},{19,11},{27,19},{20,... | collective-permute-start | bytes 786440 | tf_op jit(solution)/shard_map/ppermute | solution.py:86
  957.2 34.3 %collective-permute-start.94 = (bf16[512,256]{1,0:T(8,128)(2,1)S(1)}, bf16[512,256]{1,0:T(8,128)(2,1)S(1)}, u32[]{:S(2)}, u32[]{:S(2)}) collective-permute-start(bf16[512,256]{1,0:T(8,128)(2,1)S(1)} %get-tuple-element.110), channel_id=1, source_target_pairs={{16,8},{24,16},{17,9},{25,17},{18,10},{26,18},{19,11},{27,19},{20,... | collective-permute-start | bytes 786440 | tf_op jit(solution)/shard_map/ppermute | solution.py:86
  958.7 34.9 %collective-permute-start.68 = (bf16[512,256]{1,0:T(8,128)(2,1)S(1)}, bf16[512,256]{1,0:T(8,128)(2,1)S(1)}, u32[]{:S(2)}, u32[]{:S(2)}) collective-permute-start(bf16[512,256]{1,0:T(8,128)(2,1)S(1)} %get-tuple-element.113), channel_id=1, source_target_pairs={{0,8},{8,16},{16,24},{1,9},{9,17},{17,25},{2,10},{10,18},{18,26},{... | collective-permute-start | bytes 786440 | tf_op jit(solution)/shard_map/ppermute | solution.py:85
  1000.9 66.3 %all-to-all-start.5 = ((bf16[4,128,1,256]{3,1,2,0:T(8,128)(2,1)}), bf16[4,128,1,256]{3,1,2,0:T(8,128)(2,1)S(1)}, u32[]{:S(2)}, u32[]{:S(2)}) async-start(bf16[4,128,1,256]{3,1,2,0:T(8,128)(2,1)} %bitcast.96), calls=%async_computation.7 | async-start | bytes 524288 | tf_op jit(solution)/shard_map/all_to_all | solution.py:252
  1004.4 42.0 %collective-permute-start.63 = (bf16[512,768]{1,0:T(8,128)(2,1)}, bf16[512,768]{1,0:T(8,128)(2,1)S(1)}, u32[]{:S(2)}, u32[]{:S(2)}) collective-permute-start(bf16[512,768]{1,0:T(8,128)(2,1)} %get-tuple-element.74), channel_id=1, source_target_pairs={{24,16},{25,17},{26,18},{27,19},{28,20},{29,21},{30,22},{31,23}} | collective-permute-start | bytes 2359304 | tf_op jit(solution)/shard_map/ppermute | solution.py:86
  1007.3 40.4 %collective-permute-start.61 = (bf16[512,768]{1,0:T(8,128)(2,1)}, bf16[512,768]{1,0:T(8,128)(2,1)S(1)}, u32[]{:S(2)}, u32[]{:S(2)}) collective-permute-start(bf16[512,768]{1,0:T(8,128)(2,1)} %add_convert_fusion.4), channel_id=1, source_target_pairs={{0,8},{8,16},{1,9},{9,17},{2,10},{10,18},{3,11},{11,19},{4,12},{12... | collective-permute-start | bytes 2359304 | tf_op jit(solution)/shard_map/ppermute | solution.py:85
  1052.4 43.7 %collective-permute-start.92 = (bf16[512,256]{1,0:T(8,128)(2,1)}, bf16[512,256]{1,0:T(8,128)(2,1)}, u32[]{:S(2)}, u32[]{:S(2)}) collective-permute-start(bf16[512,256]{1,0:T(8,128)(2,1)} %get-tuple-element.109), channel_id=1, source_target_pairs={{0,8},{8,16},{16,24},{1,9},{9,17},{17,25},{2,10},{10,18},{18,26},{... | collective-permute-start | bytes 786440 | tf_op jit(solution)/shard_map/ppermute | solution.py:85
  1058.3 33.8 %collective-permute-start.64 = (bf16[512,768]{1,0:T(8,128)(2,1)}, bf16[512,768]{1,0:T(8,128)(2,1)}, u32[]{:S(2)}, u32[]{:S(2)}) collective-permute-start(bf16[512,768]{1,0:T(8,128)(2,1)} %get-tuple-element.72), channel_id=1, source_target_pairs={{16,8},{24,16},{17,9},{25,17},{18,10},{26,18},{19,11},{27,19},{20,... | collective-permute-start | bytes 2359304 | tf_op jit(solution)/shard_map/ppermute | solution.py:86
  (317 other events, 5411.2 us)
Sparse Core Ops, SparseCore 0:
  12.8 71.2 all-gather.3
  399.1 77.9 reduce-scatter.2
  485.6 54.3 all-gather.5
  694.5 118.8 all-reduce.1
  817.2 72.0 reduce-scatter.4
